TPU v7x, 256 devices: a whole 4x4x8 slice. The times are simulated.
256 devices in a mesh: src: 8 (over x, core), rcv: 32 (over z, y).
Axes of the slice: x: 4, y: 4, z: 8, core: 2. Of those that a mesh axis runs over, the one named last changes fastest.
Arguments:
- data: bfloat16 [3, 2, 4096, 4096], P(None, None, 'src', 'rcv'), may hold values from -0.75 to 0.75
Outputs:
- predicted: bfloat16 [3, 2, 4096, 4096], P(None, None, 'src', 'rcv')
All inputs are finite; a program needn't handle non-finite values.
Results may differ from a plain program's by a relative error of at most 0.001.
Values may be sent and summed in bfloat16 or wider, within the bound.
A program may use at most 128 MiB of HBM per device.

v0:
```python
import jax
import jax.numpy as jnp
from jax import lax
from jax.sharding import PartitionSpec as P


def accumulate(left_piece, right_piece):
    left_real = left_piece[:, 0]
    left_imag = left_piece[:, 1]
    right_real = right_piece[:, 0]
    right_imag = right_piece[:, 1]

    def mult(a, b):
        return jnp.einsum("fsx,fxc->fsc", a, b, preferred_element_type=jnp.float32)

    real_part = mult(left_real, right_real) - mult(left_imag, right_imag)
    imag_part = mult(left_real, right_imag) + mult(left_imag, right_real)
    return jnp.stack([real_part, imag_part], axis=1)


def make_adder(right_full, piece):
    return accumulate(piece, right_full)


def local(data):

    def one_frequency(panel):
        block = panel[None]
        right_full = lax.all_gather(block, "src", axis=2, tiled=True)
        total = make_adder(right_full, lax.all_gather(block, "rcv", axis=3, tiled=True))
        return total[0].astype(jnp.bfloat16)

    return lax.map(one_frequency, data)


def solution(mesh):
    in_specs = (P(None, None, "src", "rcv"),)
    out_specs = P(None, None, "src", "rcv")
    return jax.shard_map(local, mesh=mesh, in_specs=in_specs, out_specs=out_specs, check_vma=False)
```

profile of v0, /device:TPU:1, one launch (start us, length us, event | category | flops | bytes accessed | tf_op | source)
XLA Modules:
  0.0 452.5 jit_solution(3823025694329698331)
XLA Ops:
  6.5 439.1 %while.10 = (s32[]{:T(128)}, bf16[3,2,512,128]{3,2,1,0:T(8,128)(2,1)}, bf16[3,2,512,128]{3,2,1,0:T(8,128)(2,1)}, s32[]{:T(128)}) while((s32[]{:T(128)}, bf16[3,2,512,128]{3,2,1,0:T(8,128)(2,1)}, bf16[3,2,512,128]{3,2,1,0:T(8,128)(2,1)}, s32[]{:T(128)}) %tuple.18), condition=%wide.region_1.2_spmd, body=%wide.region_0.1_spmd.sunk | while | flops 2148270080 | bytes 89915624 | solution.py:33
  6.5 0.0 all-gather.5.cloned.1.call-start
  6.5 1.7 constant_dynamic-slice_fusion.2
  8.2 0.0 all-gather.5.cloned.1.call-update
  8.2 0.0 all-gather.3.cloned.1.call-start
  8.3 0.7 all-gather.3.cloned.1.call-update
  9.0 32.1 %all-gather.5.cloned.1.call-done = bf16[1,2,4096,128]{3,2,1,0:T(8,128)(2,1)} async-done(((bf16[1,2,512,128]{3,2,1,0:T(8,128)(2,1)}), bf16[1,2,4096,128]{3,2,1,0:T(8,128)(2,1)}) %all-gather.5.cloned.1.call-update) | async-done | bytes 2097168 | tf_op jit(solution)/shard_map/while/body/eval_jaxpr/all_gather | solution.py:29
  41.1 103.6 %all-gather.3.cloned.1.call-done = bf16[1,2,512,4096]{3,2,1,0:T(8,128)(2,1)} async-done(((bf16[1,2,512,128]{3,2,1,0:T(8,128)(2,1)}), bf16[1,2,512,4096]{3,2,1,0:T(8,128)(2,1)}) %all-gather.3.cloned.1.call-update) | async-done | bytes 8388624 | tf_op jit(solution)/shard_map/while/body/eval_jaxpr/all_gather | solution.py:30
  144.8 3.9 fusion.16
  148.7 0.0 copy-done
  148.7 0.0 slice-start.1
  148.7 3.6 fusion.14
  152.3 0.0 slice-done
  152.3 0.0 slice-done.1
  152.3 1.3 fusion.17
  153.6 1.3 fusion.15
  154.9 0.7 maximum_dynamic-update-slice_fusion.2
  155.6 0.0 all-gather.5.cloned.1.call-start
  155.6 1.7 constant_dynamic-slice_fusion.2
  157.3 0.0 all-gather.5.cloned.1.call-update
  157.3 0.0 all-gather.3.cloned.1.call-start
  157.4 0.5 all-gather.3.cloned.1.call-update
  157.9 28.6 %all-gather.5.cloned.1.call-done = bf16[1,2,4096,128]{3,2,1,0:T(8,128)(2,1)} async-done(((bf16[1,2,512,128]{3,2,1,0:T(8,128)(2,1)}), bf16[1,2,4096,128]{3,2,1,0:T(8,128)(2,1)}) %all-gather.5.cloned.1.call-update) | async-done | bytes 2097168 | tf_op jit(solution)/shard_map/while/body/eval_jaxpr/all_gather | solution.py:29
  186.5 103.5 %all-gather.3.cloned.1.call-done = bf16[1,2,512,4096]{3,2,1,0:T(8,128)(2,1)} async-done(((bf16[1,2,512,128]{3,2,1,0:T(8,128)(2,1)}), bf16[1,2,512,4096]{3,2,1,0:T(8,128)(2,1)}) %all-gather.3.cloned.1.call-update) | async-done | bytes 8388624 | tf_op jit(solution)/shard_map/while/body/eval_jaxpr/all_gather | solution.py:30
  289.9 3.9 fusion.16
  293.8 0.0 copy-done
  293.8 0.0 slice-start.1
  293.9 3.6 fusion.14
  297.4 0.0 slice-done
  297.4 0.0 slice-done.1
  297.5 1.3 fusion.17
  298.7 1.3 fusion.15
  300.0 0.7 maximum_dynamic-update-slice_fusion.2
  300.8 0.0 all-gather.5.cloned.1.call-start
  300.8 1.7 constant_dynamic-slice_fusion.2
  302.4 0.0 all-gather.5.cloned.1.call-update
  302.5 0.0 all-gather.3.cloned.1.call-start
  302.5 0.5 all-gather.3.cloned.1.call-update
  303.0 28.3 %all-gather.5.cloned.1.call-done = bf16[1,2,4096,128]{3,2,1,0:T(8,128)(2,1)} async-done(((bf16[1,2,512,128]{3,2,1,0:T(8,128)(2,1)}), bf16[1,2,4096,128]{3,2,1,0:T(8,128)(2,1)}) %all-gather.5.cloned.1.call-update) | async-done | bytes 2097168 | tf_op jit(solution)/shard_map/while/body/eval_jaxpr/all_gather | solution.py:29
  331.3 103.5 %all-gather.3.cloned.1.call-done = bf16[1,2,512,4096]{3,2,1,0:T(8,128)(2,1)} async-done(((bf16[1,2,512,128]{3,2,1,0:T(8,128)(2,1)}), bf16[1,2,512,4096]{3,2,1,0:T(8,128)(2,1)}) %all-gather.3.cloned.1.call-update) | async-done | bytes 8388624 | tf_op jit(solution)/shard_map/while/body/eval_jaxpr/all_gather | solution.py:30
  434.8 3.9 fusion.16
  438.7 0.0 slice-start.1
  438.7 3.6 fusion.14
  442.3 0.0 slice-done
  442.3 0.0 slice-done.1
  442.3 1.3 fusion.17
  443.6 1.3 fusion.15
  444.9 0.7 maximum_dynamic-update-slice_fusion.2
  (11 shorter events, 0.0 us)
Async XLA Ops:
  6.5 34.6 %all-gather.5.cloned.1.call-start = ((), (), s32[]{:S(2)}) async-start(), calls=%async_computation.1 | async-start | bytes 2359296 | tf_op jit(solution)/shard_map/while/body/eval_jaxpr/all_gather | solution.py:29
  8.2 136.5 %all-gather.3.cloned.1.call-start = ((), (), s32[]{:S(2)}) async-start(), calls=%async_computation | async-start | bytes 8650752 | tf_op jit(solution)/shard_map/while/body/eval_jaxpr/all_gather | solution.py:30
  41.1 107.5 %copy-start = (bf16[1,2,4096,128]{3,2,1,0:T(8,128)(2,1)S(1)}, bf16[1,2,4096,128]{3,2,1,0:T(8,128)(2,1)}, u32[]{:S(2)}) copy-start(bf16[1,2,4096,128]{3,2,1,0:T(8,128)(2,1)} %all-gather.5.cloned.1.call-done) | copy-start | bytes 6291460 | tf_op jit(solution)/shard_map/while
  144.8 7.5 %slice-start = ((s8[8388608]{0:T(1024)(128)(4,1)}), s8[4194304]{0:T(1024)(128)(4,1)S(1)}, s32[]{:S(2)}) async-start(s8[8388608]{0:T(1024)(128)(4,1)} %bitcast.52), calls=%async_computation.2 | async-start | bytes 8388608 | tf_op jit(solution)/shard_map/while
  148.7 3.6 slice-start.1
  155.6 30.9 %all-gather.5.cloned.1.call-start = ((), (), s32[]{:S(2)}) async-start(), calls=%async_computation.1 | async-start | bytes 2359296 | tf_op jit(solution)/shard_map/while/body/eval_jaxpr/all_gather | solution.py:29
  157.3 132.6 %all-gather.3.cloned.1.call-start = ((), (), s32[]{:S(2)}) async-start(), calls=%async_computation | async-start | bytes 8650752 | tf_op jit(solution)/shard_map/while/body/eval_jaxpr/all_gather | solution.py:30
  186.5 107.4 %copy-start = (bf16[1,2,4096,128]{3,2,1,0:T(8,128)(2,1)S(1)}, bf16[1,2,4096,128]{3,2,1,0:T(8,128)(2,1)}, u32[]{:S(2)}) copy-start(bf16[1,2,4096,128]{3,2,1,0:T(8,128)(2,1)} %all-gather.5.cloned.1.call-done) | copy-start | bytes 6291460 | tf_op jit(solution)/shard_map/while
  289.9 7.5 %slice-start = ((s8[8388608]{0:T(1024)(128)(4,1)}), s8[4194304]{0:T(1024)(128)(4,1)S(1)}, s32[]{:S(2)}) async-start(s8[8388608]{0:T(1024)(128)(4,1)} %bitcast.52), calls=%async_computation.2 | async-start | bytes 8388608 | tf_op jit(solution)/shard_map/while
  293.8 3.6 slice-start.1
  300.8 30.5 %all-gather.5.cloned.1.call-start = ((), (), s32[]{:S(2)}) async-start(), calls=%async_computation.1 | async-start | bytes 2359296 | tf_op jit(solution)/shard_map/while/body/eval_jaxpr/all_gather | solution.py:29
  302.5 132.3 %all-gather.3.cloned.1.call-start = ((), (), s32[]{:S(2)}) async-start(), calls=%async_computation | async-start | bytes 8650752 | tf_op jit(solution)/shard_map/while/body/eval_jaxpr/all_gather | solution.py:30
  331.3 107.4 %copy-start = (bf16[1,2,4096,128]{3,2,1,0:T(8,128)(2,1)S(1)}, bf16[1,2,4096,128]{3,2,1,0:T(8,128)(2,1)}, u32[]{:S(2)}) copy-start(bf16[1,2,4096,128]{3,2,1,0:T(8,128)(2,1)} %all-gather.5.cloned.1.call-done) | copy-start | bytes 6291460 | tf_op jit(solution)/shard_map/while
  434.8 7.5 %slice-start = ((s8[8388608]{0:T(1024)(128)(4,1)}), s8[4194304]{0:T(1024)(128)(4,1)S(1)}, s32[]{:S(2)}) async-start(s8[8388608]{0:T(1024)(128)(4,1)} %bitcast.52), calls=%async_computation.2 | async-start | bytes 8388608 | tf_op jit(solution)/shard_map/while
  438.7 3.6 slice-start.1
Sparse Core Ops, SparseCore 0:
  9.2 31.9 all-gather.4
  43.6 101.1 all-gather.2
  158.3 28.1 all-gather.4
  188.8 101.1 all-gather.2
  303.1 28.1 all-gather.4
  333.6 101.1 all-gather.2
where the time goes:
time: 454 us; the launch traced here: 452 us
  waiting for transfers between devices  401 us (88%)
  matrix products  30.1 us (7%)
  between operations  13.4 us (3%)
  local copies, waits for them, and re-layouts  5.07 us (1%)
    all_gather x3, waiting for transfers between devices, one_frequency(): lax.all_gather(block, 'rcv', axis=3, tiled=True)  311 us
    all_gather x3, waiting for transfers between devices, one_frequency(): right_full = lax.all_gather(block, 'src', axis=2, tiled=True)  89 us
    dot_general x12, matrix products, mult(): return jnp.einsum('fsx,fxc->fsc', a, b, preferred_element_type=jnp.float32)  30.1 us
  transfers between devices with their start and end apart: 6, of which 6 were waited for; matrix products, arithmetic and copies ran while one was open for 0% of the time, Pallas kernels for 0%

commit v1 on v0

v1 whole, which is shorter than its diff:
```python
import functools

import jax
import jax.numpy as jnp
from jax import lax
from jax.experimental import pallas as pl
from jax.experimental.pallas import tpu as pltpu
from jax.sharding import PartitionSpec as P

MESH = pl.DeviceIdType.MESH
NX, NY, NZ = 4, 4, 8
ROWS, COLS = 512, 128
HALF = ROWS // 2
PARTS = 2
PIECE = ROWS // PARTS
ORDER = ((0, 0), (1, 1), (0, 1), (1, 0))


def hops(direction, unit):
    return 4 if direction == unit else 3


def kernel(d, o, left_a, right_a, left_b, right_b, acc_a, acc_b, part, out_a, out_b,
           own_left_s, own_left_r, own_right_s, own_right_r, own_a_s, own_a_r, local_sem,
           zb_s, zb_r, za_s, za_r, cb_s, cb_r, ca_s, ca_r, xb_s, xb_r, xa_s, xa_r,
           part_s, part_r, fin_a_s, fin_a_r, fin_b_s, fin_b_r):
    src, rcv = lax.axis_index("src"), lax.axis_index("rcv")
    x, c = src // 2, src % 2
    z, y = rcv // NY, rcv % NY
    h, low = y // 2, y % 2

    def dev(x, c, z, y):
        return (x * 2 + c, z * NY + y)

    z_next = (dev(x, c, (z + 1) % NZ, y), dev(x, c, (z + NZ - 1) % NZ, y))
    x_next = (dev((x + 1) % NX, c, z, y), dev((x + NX - 1) % NX, c, z, y))
    partner = dev(x, 1 - c, z, y)

    barrier = pltpu.get_barrier_semaphore()
    friends = list(z_next) + list(x_next) + [partner]
    for step in range(1, NY):
        for core in range(2):
            friends.append(dev(x, (c + core) % 2, z, (y + step) % NY))
    for friend in friends:
        pl.semaphore_signal(barrier, inc=1, device_id=friend, device_id_type=MESH)
    pl.semaphore_wait(barrier, len(friends))

    sent = []

    def send(src_ref, dst_ref, s_sem, r_sem, device, here=None):
        copy = pltpu.make_async_remote_copy(
            src_ref=src_ref, dst_ref=dst_ref, send_sem=s_sem, recv_sem=r_sem, device_id=device, device_id_type=MESH)
        if here is None:
            copy.start()
        else:
            pl.when(jnp.logical_not(here))(copy.start)
            pl.when(here)(pltpu.make_async_copy(src_ref, dst_ref, r_sem).start)
        sent.append((copy, here))

    def got(dst_ref, r_sem):
        pltpu.make_async_copy(dst_ref, dst_ref, r_sem).wait()

    def piece(q):
        return pl.ds(q * PIECE, PIECE)

    for u in range(2):
        send(d.at[1, u], left_b.at[z, low, u], own_left_s.at[u], own_left_r.at[u], dev(x, low, z, h * 2 + c), low == c)
    for half in range(2):
        for k in range(2):
            send(d.at[1, :, pl.ds(half * HALF, HALF)], right_b.at[x, c, low], own_right_s.at[half, k], own_right_r.at[c, low],
                 dev(x, h, z, half * 2 + k), jnp.logical_and(h == c, y == half * 2 + k))

    def block_b(zz, u, q):
        return left_b.at[zz, c, u, piece(q)]

    def block_a(zz, u, q):
        return left_a.at[zz, 2 * c + u, :, piece(q)]

    def own_a(u, q):
        return right_a.at[x, low, u, :, piece(q)]

    def z_first(block, source, s_sem, r_sem, c_s, c_r):
        for q in range(PARTS):
            for direction, u in ORDER:
                send(source(u, q), block(z, u, q), s_sem.at[direction, 0, u, q], r_sem.at[direction, 0, u, q], z_next[direction])
            for u in range(2):
                send(source(u, q), block(z, u, q), c_s.at[0, u, q], c_r.at[0, u, q], partner)

    def come(direction, step):
        return (z + NZ - step) % NZ if direction == 0 else (z + step) % NZ

    def away(direction, step):
        return (NZ - step) % NZ if direction == 0 else step

    def z_arrive(block, s_sem, r_sem, c_s, c_r, step, parts=range(PARTS)):
        for q in parts:
            for direction, u in ORDER:
                if step > hops(direction, u):
                    continue
                here = block(come(direction, step), u, q)
                got(here, r_sem.at[direction, step - 1, u, q])
                if step < hops(direction, u):
                    send(here, here, s_sem.at[direction, step, u, q], r_sem.at[direction, step, u, q], z_next[direction])
                k = away(direction, step)
                send(here, here, c_s.at[k, u, q], c_r.at[k, u, q], partner)

    def c_arrive(wide, c_r, k, parts=range(PARTS)):
        for q in parts:
            for u in range(2):
                got(wide((z + k) % NZ, u, q), c_r.at[k, u, q])

    def other_b(zz, u, q):
        return left_b.at[zz, 1 - c, u, piece(q)]

    def other_a(zz, u, q):
        return left_a.at[zz, 2 * (1 - c) + u, :, piece(q)]

    zb = (zb_s, zb_r, cb_s, cb_r)
    za = (za_s, za_r, ca_s, ca_r)

    def x_first(right, s_sem, r_sem):
        for k in range(2):
            for p in range(2):
                for direction in range(2):
                    send(right.at[x, k, p], right.at[x, k, p], s_sem.at[direction, 0, k, p], r_sem.at[direction, 0, k, p], x_next[direction])

    def x_second(right, s_sem, r_sem):
        for k in range(2):
            for p in range(2):
                for direction in range(2):
                    xx = (x + NX - 1) % NX if direction == 0 else (x + 1) % NX
                    here = right.at[xx, k, p]
                    got(here, r_sem.at[direction, 0, k, p])
                    if p == direction:
                        send(here, here, s_sem.at[direction, 1, k, p], r_sem.at[direction, 1, k, p], x_next[direction])

    def x_last(right, r_sem):
        for k in range(2):
            for direction in range(2):
                got(right.at[(x + 2) % NX, k, direction], r_sem.at[direction, 1, k, direction])

    def multiply(left, width, right, acc, zz, q, rows):
        xx, k = zz // 2, zz % 2
        at = pl.ds(q * rows, rows)
        lr = jnp.concatenate([left[zz, j, 0, at, :] for j in range(width)], axis=1)
        li = jnp.concatenate([left[zz, j, 1, at, :] for j in range(width)], axis=1)
        rr = jnp.concatenate([right[xx, k, p, 0] for p in range(2)], axis=1)
        ri = jnp.concatenate([right[xx, k, p, 1] for p in range(2)], axis=1)

        def dot(a, b):
            return jnp.dot(a, b, preferred_element_type=jnp.float32)

        acc[0, at, :] += dot(lr, rr) - dot(li, ri)
        acc[1, at, :] += dot(lr, ri) + dot(li, rr)

    for u in range(2):
        got(left_b.at[z, c, u], own_left_r.at[u])
    z_first(block_b, lambda u, q: block_b(z, u, q), *zb)
    for k in range(2):
        for p in range(2):
            got(right_b.at[x, k, p], own_right_r.at[k, p])
    x_first(right_b, xb_s, xb_r)
    for half in range(2):
        for k in range(2):
            send(d.at[2 * half], right_a.at[x, c, low], own_a_s.at[half, k], own_a_r.at[c, low],
                 dev(x, h, z, half * 2 + k), jnp.logical_and(h == c, y == half * 2 + k))
    acc_a[...] = jnp.zeros_like(acc_a)
    acc_b[...] = jnp.zeros_like(acc_b)
    z_arrive(block_b, *zb, 1)
    x_second(right_b, xb_s, xb_r)
    z_arrive(block_b, *zb, 2)
    for k in range(2):
        for p in range(2):
            got(right_a.at[x, k, p], own_a_r.at[k, p])
    z_first(block_a, own_a, *za)
    x_first(right_a, xa_s, xa_r)
    keep = pltpu.make_async_copy(right_a.at[x, low], left_a.at[z, pl.ds(2 * c, 2)], local_sem)
    keep.start()
    z_arrive(block_b, *zb, 3)
    z_arrive(block_b, *zb, 4)
    x_last(right_b, xb_r)
    for k in range(NZ):
        c_arrive(other_b, cb_r, k)

    def whole_b(k, _):
        for q in range(2):
            multiply(left_b, 2, right_b, acc_b, (z + k) % NZ, q, HALF)
        return 0

    lax.fori_loop(0, NZ, whole_b, 0)
    send(acc_b.at[:, pl.ds((1 - h) * HALF, HALF)], part, part_s, part_r, dev(x, c, z, (y + 2) % NY))
    z_arrive(block_a, *za, 1)
    x_second(right_a, xa_s, xa_r)
    got(part, part_r)
    for p in range(2):
        for i in range(2):
            at = pl.ds(p * COLS, COLS)
            out_b[p, i] = (acc_b[i, pl.ds(pl.multiple_of(h * HALF, HALF), HALF), at] + part[i, :, at]).astype(jnp.bfloat16)
        send(out_b.at[p], o.at[1, :, pl.ds(h * HALF, HALF)], fin_b_s.at[p], fin_b_r.at[h],
             dev(x, low, z, 2 * c + p), jnp.logical_and(low == c, y == 2 * c + p))
    z_arrive(block_a, *za, 2)
    z_arrive(block_a, *za, 3)
    keep.wait()
    x_last(right_a, xa_r)
    for k in range(NZ):
        if k != 4:
            c_arrive(other_a, ca_r, k)

    def whole_a(k, _):
        for q in range(2):
            multiply(left_a, 4, right_a, acc_a, (z + k + 5) % NZ, q, HALF)
        return 0

    lax.fori_loop(0, NZ - 1, whole_a, 0)
    for q in range(PARTS):
        z_arrive(block_a, *za, 4, (q,))
        c_arrive(other_a, ca_r, 4, (q,))
        multiply(left_a, 4, right_a, acc_a, (z + 4) % NZ, q, PIECE)
        for p in range(2):
            for i in range(2):
                out_a[p, i, piece(q)] = acc_a[i, piece(q), pl.ds(p * COLS, COLS)].astype(jnp.bfloat16)
            send(out_a.at[p, :, piece(q)], o.at[2 * h, :, piece(q)], fin_a_s.at[p, q], fin_a_r.at[h, q],
                 dev(x, low, z, 2 * c + p), jnp.logical_and(low == c, y == 2 * c + p))
    for half in range(2):
        got(o.at[1, :, pl.ds(half * HALF, HALF)], fin_b_r.at[half])
        for q in range(PARTS):
            got(o.at[2 * half, :, piece(q)], fin_a_r.at[half, q])
    for copy, here in sent:
        if here is None:
            copy.wait_send()
        else:
            pl.when(jnp.logical_not(here))(copy.wait_send)


def local(data):
    bf16, f32 = jnp.bfloat16, jnp.float32
    sem = pltpu.SemaphoreType.DMA
    return pl.pallas_call(
        kernel,
        out_shape=jax.ShapeDtypeStruct(data.shape, data.dtype),
        in_specs=[pl.BlockSpec(memory_space=pltpu.VMEM)],
        out_specs=pl.BlockSpec(memory_space=pltpu.VMEM),
        scratch_shapes=[
            pltpu.VMEM((NZ, 4, 2, ROWS, COLS), bf16),
            pltpu.VMEM((NX, 2, 2, 2, ROWS, COLS), bf16),
            pltpu.VMEM((NZ, 2, 2, ROWS, COLS), bf16),
            pltpu.VMEM((NX, 2, 2, 2, HALF, COLS), bf16),
            pltpu.VMEM((2, ROWS, 2 * COLS), f32),
            pltpu.VMEM((2, ROWS, 2 * COLS), f32),
            pltpu.VMEM((2, HALF, 2 * COLS), f32),
            pltpu.VMEM((2, 2, ROWS, COLS), bf16),
            pltpu.VMEM((2, 2, HALF, COLS), bf16),
            sem((2,)), sem((2,)),
            sem((2, 2)), sem((2, 2)),
            sem((2, 2)), sem((2, 2)),
            sem,
            sem((2, 4, 2, PARTS)), sem((2, 4, 2, PARTS)),
            sem((2, 4, 2, PARTS)), sem((2, 4, 2, PARTS)),
            sem((NZ, 2, PARTS)), sem((NZ, 2, PARTS)),
            sem((NZ, 2, PARTS)), sem((NZ, 2, PARTS)),
            sem((2, 2, 2, 2)), sem((2, 2, 2, 2)),
            sem((2, 2, 2, 2)), sem((2, 2, 2, 2)),
            sem, sem,
            sem((2, PARTS)), sem((2, PARTS)),
            sem((2,)), sem((2,)),
        ],
        compiler_params=pltpu.CompilerParams(collective_id=0, has_side_effects=True, vmem_limit_bytes=48 << 20),
        cost_estimate=pl.CostEstimate(flops=6442450944, bytes_accessed=1572864, transcendentals=0),
    )(data)


def solution(mesh):
    spec = P(None, None, "src", "rcv")
    return jax.shard_map(local, mesh=mesh, in_specs=(spec,), out_specs=spec, check_vma=False)
```

time: 454 us -> 108 us (0.24)
  waiting for transfers between devices: 401 us -> 0 us
  Pallas kernels: 0 us -> 106 us
  matrix products: 30.1 us -> 0 us
  between operations: 13.4 us -> 0.01 us
    all_gather x6 -> x0, waiting for transfers between devices: 400 us -> none  [the longest x3 311 us: one_frequency(): lax.all_gather(block, 'rcv', axis=3, tiled=True)]
    pallas_call x0 -> x1, Pallas kernels: none -> 106 us  [local(): pl.pallas_call(kernel, out_shape=jax.ShapeDtypeStruct(data.shape, data.dt...]
    dot_general x12 -> x0, matrix products: 30.1 us -> none  [mult(): return jnp.einsum('fsx,fxc->fsc', a, b, preferred_element_type=jnp.float32)]
    dynamic_slice x3 -> x0, local copies, waits for them, and re-layouts: 5.04 us -> none  [local(): return lax.map(one_frequency, data)]
  transfers between devices with their start and end apart: 6 -> 0, of which waited for: 6 -> 0; matrix products, arithmetic and copies ran while one was open for 0% -> 0% of each run, Pallas kernels for 0% -> 0%
where the time goes in v1:
time: 108 us
  Pallas kernels  106 us (98%)
  local copies, waits for them, and re-layouts  2.01 us (2%)
    pallas_call x1, Pallas kernels, local(): pl.pallas_call(kernel, out_shape=jax.ShapeDtypeStruct(data.shape, data.dt...  106 us

profile of v1, /device:TPU:1, one launch (start us, length us, event | category | flops | bytes accessed | tf_op | source)
XLA Modules:
  0.0 108.2 jit_solution(3747908713283424350)
XLA Ops:
  0.0 0.0 copy-start
  0.0 1.1 %copy-done = bf16[3,2,512,128]{3,2,1,0:T(8,128)(2,1)S(1)} copy-done((bf16[3,2,512,128]{3,2,1,0:T(8,128)(2,1)S(1)}, bf16[3,2,512,128]{3,2,1,0:T(8,128)(2,1)}, u32[]{:S(2)}) %copy-start) | copy-done | bytes 786456
  1.1 106.2 %shard_map.17 = bf16[3,2,512,128]{3,2,1,0:T(8,128)(2,1)S(1)} custom-call(bf16[3,2,512,128]{3,2,1,0:T(8,128)(2,1)S(1)} %copy-done), custom_call_target="tpu_custom_call" | custom-call | flops 6442450944 | bytes 1572864 | tf_op jit(solution)/shard_map/pallas_call | solution.py:238
  107.3 0.9 copy.3
Async XLA Ops:
  0.0 1.1 %copy-start = (bf16[3,2,512,128]{3,2,1,0:T(8,128)(2,1)S(1)}, bf16[3,2,512,128]{3,2,1,0:T(8,128)(2,1)}, u32[]{:S(2)}) copy-start(bf16[3,2,512,128]{3,2,1,0:T(8,128)(2,1)} %d.1) | copy-start | bytes 2359300

commit v2 on v0

v2 whole, which is shorter than its diff:
```python
import functools

import jax
import jax.numpy as jnp
from jax import lax
from jax.experimental import pallas as pl
from jax.experimental.pallas import tpu as pltpu
from jax.sharding import PartitionSpec as P

MESH = pl.DeviceIdType.MESH
NX, NY, NZ = 4, 4, 8
ROWS, COLS = 512, 128
HALF = ROWS // 2
PARTS = 2
PIECE = ROWS // PARTS


def hops(direction, n):
    return 4 if direction == n else 3


def kernel(d, o, left_a, right_a, left_b, right_b, acc_a, acc_b, part, out_a, out_b,
           own_left_s, own_left_r, own_b_s, own_b_r, own_a_s, own_a_r, give_s, give_r, keep_sem,
           zb_s, zb_r, za_s, za_r, cb_s, cb_r, ca_s, ca_r, xb_s, xb_r, xa_s, xa_r, tb_s, tb_r, ta_s, ta_r,
           part_s, part_r, fin_a_s, fin_a_r, fin_b_s, fin_b_r):
    src, rcv = lax.axis_index("src"), lax.axis_index("rcv")
    x, c = src // 2, src % 2
    z, y = rcv // NY, rcv % NY
    h = y // 2
    low = (y + h) % 2
    pair, across = 2 * h + (y + 1) % 2, NY - 1 - y

    def dev(x, c, z, y):
        return (x * 2 + c, z * NY + y)

    z_next = (dev(x, c, (z + 1) % NZ, y), dev(x, c, (z + NZ - 1) % NZ, y))
    x_next = (dev((x + 1) % NX, c, z, y), dev((x + NX - 1) % NX, c, z, y))
    partner = dev(x, 1 - c, z, y)

    barrier = pltpu.get_barrier_semaphore()
    friends = list(z_next) + list(x_next) + [partner]
    for step in range(1, NY):
        for core in range(2):
            friends.append(dev(x, (c + core) % 2, z, (y + step) % NY))
    for friend in friends:
        pl.semaphore_signal(barrier, inc=1, device_id=friend, device_id_type=MESH)
    acc_a[...] = jnp.zeros_like(acc_a)
    acc_b[...] = jnp.zeros_like(acc_b)
    pl.semaphore_wait(barrier, len(friends))

    def piece(q):
        return pl.ds(q * PIECE, PIECE)

    def got(dst_ref, r_sem):
        pltpu.make_async_copy(dst_ref, dst_ref, r_sem).wait()

    def send(sent, src_ref, dst_ref, s_sem, r_sem, device, here=None):
        copy = pltpu.make_async_remote_copy(
            src_ref=src_ref, dst_ref=dst_ref, send_sem=s_sem, recv_sem=r_sem, device_id=device, device_id_type=MESH)
        if here is None:
            copy.start()
        else:
            pl.when(jnp.logical_not(here))(copy.start)
            pl.when(here)(pltpu.make_async_copy(src_ref, dst_ref, r_sem).start)
        sent.append((copy, here))

    def all_sent(sent):
        for copy, here in sent:
            if here is None:
                copy.wait_send()
            else:
                pl.when(jnp.logical_not(here))(copy.wait_send)

    first = []
    stays = low == c
    send(first, d.at[1, :, pl.ds((1 - h) * HALF, HALF)], right_b.at[x, c, y], own_b_s.at[0, 1, 0], own_b_r.at[0, c, 1], dev(x, 1, z, across))
    for q in range(PARTS):
        send(first, d.at[1, :, piece(q)], left_b.at[z, y % 2, :, piece(q)], own_left_s.at[q], own_left_r.at[jnp.where(stays, 0, 1), q],
             dev(x, 0, z, jnp.where(stays, y, pair)), jnp.logical_and(stays, c == 0))
    send(first, d.at[1, :, pl.ds(h * HALF, HALF)], right_b.at[x, c, y], own_b_s.at[0, 0, 0], own_b_r.at[0, c, 0], dev(x, 1, z, y), c == 1)
    send(first, d.at[2 * (1 - h)], right_a.at[x, c, y], own_a_s.at[0, 1, 0], own_a_r.at[0, c, 1], dev(x, 1, z, across))
    send(first, d.at[2 * h], right_a.at[x, c, y], own_a_s.at[0, 0, 0], own_a_r.at[0, c, 0], dev(x, 1, z, y), c == 1)

    def column(n, m):
        base = y if n == 0 else pair
        return base if m == 0 else NY - 1 - base

    def low_column(n):
        near = jnp.where(h == 0, y, across)
        return near if n == 0 else 1 - near

    def block_b(zz, n, m, q):
        return left_b.at[zz, (y + n) % 2, :, piece(q)]

    def block_a(zz, n, m, q):
        return left_a.at[zz, column(n, m), :, piece(q)]

    zb = (block_b, 1, zb_s, zb_r, cb_s, cb_r)
    za = (block_a, 2, za_s, za_r, ca_s, ca_r)
    xb = (right_b, xb_s, xb_r, tb_s, tb_r)
    xa = (right_a, xa_s, xa_r, ta_s, ta_r)

    def run(core):
        sent = []
        give = functools.partial(send, sent)
        plan = []

        def at_time(time, action, *args):
            plan.append((time, functools.partial(action, *args)))

        def z_first(block, ms, s_sem, r_sem, c_s, c_r, n, m, q, back):
            here = block(z, n, m, q)
            for direction in range(2):
                give(here, here, s_sem.at[direction, 0, n, m, q], r_sem.at[direction, 0, n, m, q], z_next[direction])
            if back:
                give(here, here, c_s.at[0, n, m, q], c_r.at[0, n, m, q], partner)

        def z_arrive(block, ms, s_sem, r_sem, c_s, c_r, step, i, m, q):
            for direction in range(2):
                n = direction if i == 0 else 1 - direction
                zz = (z + NZ - step) % NZ if direction == 0 else (z + step) % NZ
                k = NZ - step if direction == 0 else step
                here = block(zz, n, m, q)
                got(here, r_sem.at[direction, step - 1, n, m, q])
                if step < hops(direction, n):
                    give(here, here, s_sem.at[direction, step, n, m, q], r_sem.at[direction, step, n, m, q], z_next[direction])
                give(here, here, c_s.at[k, n, m, q], c_r.at[k, n, m, q], partner)

        def start_b(n):
            for q in range(PARTS):
                got(block_b(z, n, 0, q), own_left_r.at[n, q])
                z_first(*zb, n, 0, q, True)

        def take_a(n, m):
            got(left_a.at[z, column(n, m)], give_r.at[n, m])

        def start_a(n, q):
            for m in range(2):
                z_first(*za, n, m, q, False)

        def left_ready(z_of, k, q):
            block, ms, _, _, _, c_r = z_of
            if core == 1 and (k or ms == 1):
                for n in range(2):
                    for m in range(ms):
                        got(block((z + k) % NZ, n, m, q), c_r.at[k, n, m, q])

        def own_second(right, s_sem, r_sem, k, m):
            here = right.at[x, k, column(0, m)]
            got(here, r_sem.at[0, k, m])
            give(here, here, s_sem.at[1, k, m], r_sem.at[1, k, m], dev(x, c, z, pair))

        def own_last(right, r_sem, k, m):
            got(right.at[x, k, column(1, m)], r_sem.at[1, k, m])

        def pass_on(right, t_s, t_r, slot, xx, k, n):
            here = right.at[xx, k, low_column(n)]
            give(here, here, t_s.at[slot, k, n], t_r.at[slot, k, n], partner)

        def x_first(right, s_sem, r_sem, t_s, t_r, n, m):
            for k in range(2):
                here = right.at[x, k, column(n, m)]
                for direction in range(2):
                    give(here, here, s_sem.at[direction, 0, k, n, m], r_sem.at[direction, 0, k, n, m], x_next[direction])
                if m == 1:
                    pass_on(right, t_s, t_r, 0, x, k, n)

        def x_arrive(right, s_sem, r_sem, t_s, t_r, k, n, m):
            for direction in range(2):
                xx = (x + NX - 1) % NX if direction == 0 else (x + 1) % NX
                here = right.at[xx, k, column(n, m)]
                got(here, r_sem.at[direction, 0, k, n, m])
                if n == direction:
                    give(here, here, s_sem.at[direction, 1, k, n, m], r_sem.at[direction, 1, k, n, m], x_next[direction])
                if m == 1:
                    pass_on(right, t_s, t_r, 1 + direction, xx, k, n)

        def x_last(right, s_sem, r_sem, t_s, t_r, k, m):
            xx = (x + 2) % NX
            for n in range(2):
                got(right.at[xx, k, column(n, m)], r_sem.at[n, 1, k, n, m])
                if m == 1:
                    pass_on(right, t_s, t_r, 3, xx, k, n)

        def give_left(n, m):
            here, there = right_a.at[x, low, column(n, m)], left_a.at[z, column(n, m)]
            give(here, there, give_s.at[n, m], give_r.at[n, m], partner)
            pltpu.make_async_copy(here, there, keep_sem.at[n, m]).start()

        def keep_left():
            for n in range(2):
                for m in range(2):
                    got(left_a.at[z, column(n, m)], keep_sem.at[n, m])

        def right_ready(x_of, slots):
            if core == 0:
                right, _, _, _, t_r = x_of
                for slot in slots:
                    for k in range(2):
                        for n in range(2):
                            got(right.at[(x + (0, 3, 1, 2)[slot]) % NX, k, low_column(n)], t_r.at[slot, k, n])

        def multiply(left, width, right, acc, zz, start, rows):
            xx, k = zz // 2, zz % 2
            at = pl.ds(start, rows)
            lr = jnp.concatenate([left[zz, j, 0, at, :] for j in range(width)], axis=1)
            li = jnp.concatenate([left[zz, j, 1, at, :] for j in range(width)], axis=1)
            rr = jnp.concatenate([right[xx, k, 2 * core + p, 0] for p in range(2)], axis=1)
            ri = jnp.concatenate([right[xx, k, 2 * core + p, 1] for p in range(2)], axis=1)

            def dot(a, b):
                return jnp.dot(a, b, preferred_element_type=jnp.float32)

            acc[0, at, :] += dot(lr, rr) - dot(li, ri)
            acc[1, at, :] += dot(lr, ri) + dot(li, rr)

        def whole_b():
            for k in range(NZ):
                for q in range(PARTS):
                    left_ready(zb, k, q)
            right_ready(xb, range(4))

            def one(k, _):
                for q in range(2):
                    multiply(left_b, 2, right_b, acc_b, (z + k) % NZ, q * HALF, HALF)
                return 0

            lax.fori_loop(0, NZ, one, 0)
            give(acc_b.at[:, pl.ds((1 - h) * HALF, HALF)], part, part_s, part_r, dev(x, c, z, across))

        def finish_b():
            got(part, part_r)
            for p in range(2):
                for i in range(2):
                    at = pl.ds(p * COLS, COLS)
                    out_b[p, i] = (acc_b[i, pl.ds(pl.multiple_of(h * HALF, HALF), HALF), at] + part[i, :, at]).astype(jnp.bfloat16)
                give(out_b.at[p], o.at[1, :, pl.ds(h * HALF, HALF)], fin_b_s.at[p], fin_b_r.at[h],
                     dev(x, low, z, 2 * c + p), jnp.logical_and(low == c, y == 2 * c + p))

        def chunks_a(start, stop, q, want=None):
            for k in range(start, stop + 1):
                left_ready(za, k % NZ, q)

            def one(k, _):
                zz = (z + k + start % NZ) % NZ
                if want is None:
                    multiply(left_a, 4, right_a, acc_a, zz, q * PIECE, PIECE)
                else:
                    far = (zz // 2 + NX - x) % NX == 2
                    pl.when(far if want else jnp.logical_not(far))(lambda: multiply(left_a, 4, right_a, acc_a, zz, q * PIECE, PIECE))
                return 0

            lax.fori_loop(0, stop + 1 - start, one, 0)

        def far_a(q):
            def one(k, _):
                multiply(left_a, 4, right_a, acc_a, ((x + 2) % NX) * 2 + k, q * PIECE, PIECE)
                return 0

            lax.fori_loop(0, 2, one, 0)

        def finish_a(q):
            for p in range(2):
                for i in range(2):
                    out_a[p, i, piece(q)] = acc_a[i, piece(q), pl.ds(p * COLS, COLS)].astype(jnp.bfloat16)
                give(out_a.at[p, :, piece(q)], o.at[2 * h, :, piece(q)], fin_a_s.at[p, q], fin_a_r.at[h, q],
                     dev(x, low, z, 2 * c + p), jnp.logical_and(low == c, y == 2 * c + p))

        hop = 1.9
        sub = 39.4 / PARTS
        begin_b = 1.7
        begin_a = begin_b + 19.7

        def z_time_b(step, i, q):
            return begin_b + 5.6 * (step - 1) + 2.8 * (i + (q + 1) / PARTS) + hop

        def z_time_a(step, i, m, q):
            if q < PARTS - 2:
                return begin_a + sub * (q + (step - 1 + (2 * i + m + 1) / 4) / 3.5) + hop
            ahead = sub / 3.5
            if q == PARTS - 2:
                return begin_a + sub * (q + (step - 1 + (2 * i + m + 1) / 4) / 3.5) + hop + (ahead if step > 1 else 0)
            if step == 1:
                return begin_a + sub * q + ahead * (1 + (2 * i + m) / 4) - 2.5
            return begin_a + sub * q + ahead * (step - 1 + (2 * i + m + 1) / 4) + hop

        if core == 0:
            at_time(1, start_b, 0)
            at_time(4.5, start_b, 1)
            for m in range(2):
                at_time(17.4 + m / 100, take_a, 0, m)
                at_time(21.5 + m / 100, take_a, 1, m)
            for q in range(PARTS):
                first_time = 0 if q == 0 else begin_a + sub * (q - 1) + 2.5
                at_time(max(17.5, first_time), start_a, 0, q)
                at_time(max(21.6, first_time + 0.01), start_a, 1, q)
            for step in range(1, 5):
                for i in range(2 if step < 4 else 1):
                    for q in range(PARTS):
                        at_time(z_time_b(step, i, q), z_arrive, *zb, step, i, 0, q)
                        for m in range(2):
                            at_time(z_time_a(step, i, m, q), z_arrive, *za, step, i, m, q)
        else:
            for k in range(2):
                at_time(1.5, own_second, right_b, own_b_s, own_b_r, k, 0)
                at_time(4.6, own_second, right_b, own_b_s, own_b_r, k, 1)
                at_time(7.6, own_last, right_b, own_b_r, k, 0)
                at_time(11, own_last, right_b, own_b_r, k, 1)
            for k in (1 - low, low):
                at_time(4.8, own_second, right_a, own_a_s, own_a_r, k, 0)
                at_time(11.2, own_second, right_a, own_a_s, own_a_r, k, 1)
            at_time(4.81, give_left, 0, 0)
            at_time(11.21, give_left, 0, 1)
            at_time(15, own_last, right_a, own_a_r, low, 0)
            at_time(15.1, give_left, 1, 0)
            at_time(17.7, own_last, right_a, own_a_r, 1 - low, 0)
            at_time(21, own_last, right_a, own_a_r, low, 1)
            at_time(21.1, give_left, 1, 1)
            at_time(23.5, own_last, right_a, own_a_r, 1 - low, 1)
            at_time(1.6, x_first, *xb, 0, 0)
            at_time(4.7, x_first, *xb, 0, 1)
            at_time(7.7, x_first, *xb, 1, 0)
            at_time(11.1, x_first, *xb, 1, 1)
            at_time(15.8, x_first, *xa, 0, 0)
            at_time(15.9, x_first, *xa, 0, 1)
            at_time(23.6, x_first, *xa, 1, 0)
            at_time(23.7, x_first, *xa, 1, 1)
            for k in range(2):
                for m in range(2):
                    nth = 2 * m + k + 1
                    at_time(2 + 1.4 * nth + hop, x_arrive, *xb, k, 0, m)
                    at_time(8 + 1.4 * nth + hop, x_arrive, *xb, k, 1, m)
                    at_time(14 + 1.4 * nth + hop, x_last, *xb, k, m)
                    at_time(19.5 + 2.8 * nth + hop, x_arrive, *xa, k, 0, m)
                    at_time(31 + 2.8 * nth + hop, x_arrive, *xa, k, 1, m)
                    at_time(42.5 + 2.8 * nth + hop, x_last, *xa, k, m)
            at_time(46.8, keep_left)
        at_time(25.2, whole_b)
        at_time(43, finish_b)
        at_time(47, right_ready, xa, range(3))
        late = 56.5
        at_time(late, right_ready, xa, (3,))
        for q in range(PARTS):
            done = z_time_a(4, 0, 1, q) + 0.2
            if done < 49:
                at_time(max(done, 47.1), chunks_a, -3, 4, q, False)
                at_time(late, far_a, q)
                at_time(late + 0.01, finish_a, q)
            elif done < late + 1:
                at_time(late + 0.02, chunks_a, -3, 4, q)
                at_time(late + 0.03, finish_a, q)
            else:
                at_time(max(late + 0.04, z_time_a(2, 1, 1, q) + 0.2), chunks_a, -2, 2, q)
                third = z_time_a(3, 1, 1, q) + 0.2
                at_time(third, chunks_a, -3, -3, q)
                at_time(third, chunks_a, 3, 3, q)
                at_time(done, chunks_a, 4, 4, q)
                at_time(done + 0.01, finish_a, q)
        for _, action in sorted(plan, key=lambda entry: entry[0]):
            action()
        all_sent(sent)

    pl.when(c == 0)(functools.partial(run, 0))
    pl.when(c == 1)(functools.partial(run, 1))
    for half in range(2):
        got(o.at[1, :, pl.ds(half * HALF, HALF)], fin_b_r.at[half])
        for q in range(PARTS):
            got(o.at[2 * half, :, piece(q)], fin_a_r.at[half, q])
    all_sent(first)


def local(data):
    bf16, f32 = jnp.bfloat16, jnp.float32
    sem = pltpu.SemaphoreType.DMA

    def sems(*shape):
        return [sem(shape), sem(shape)]

    return pl.pallas_call(
        kernel,
        out_shape=jax.ShapeDtypeStruct(data.shape, data.dtype),
        in_specs=[pl.BlockSpec(memory_space=pltpu.VMEM)],
        out_specs=pl.BlockSpec(memory_space=pltpu.VMEM),
        scratch_shapes=[
            pltpu.VMEM((NZ, 4, 2, ROWS, COLS), bf16),
            pltpu.VMEM((NX, 2, 4, 2, ROWS, COLS), bf16),
            pltpu.VMEM((NZ, 2, 2, ROWS, COLS), bf16),
            pltpu.VMEM((NX, 2, 4, 2, HALF, COLS), bf16),
            pltpu.VMEM((2, ROWS, 2 * COLS), f32),
            pltpu.VMEM((2, ROWS, 2 * COLS), f32),
            pltpu.VMEM((2, HALF, 2 * COLS), f32),
            pltpu.VMEM((2, 2, ROWS, COLS), bf16),
            pltpu.VMEM((2, 2, HALF, COLS), bf16),
            sem((PARTS,)), sem((2, PARTS)),
            *sems(2, 2, 2), *sems(2, 2, 2), *sems(2, 2), sem((2, 2)),
            *sems(2, 4, 2, 1, PARTS), *sems(2, 4, 2, 2, PARTS),
            *sems(NZ, 2, 1, PARTS), *sems(NZ, 2, 2, PARTS),
            *sems(2, 2, 2, 2, 2), *sems(2, 2, 2, 2, 2),
            *sems(4, 2, 2), *sems(4, 2, 2),
            sem, sem,
            *sems(2, PARTS), *sems(2),
        ],
        compiler_params=pltpu.CompilerParams(collective_id=0, has_side_effects=True, vmem_limit_bytes=48 << 20),
        cost_estimate=pl.CostEstimate(flops=6442450944, bytes_accessed=1572864, transcendentals=0),
    )(data)


def solution(mesh):
    spec = P(None, None, "src", "rcv")
    return jax.shard_map(local, mesh=mesh, in_specs=(spec,), out_specs=spec, check_vma=False)
```

time: 454 us -> 90.4 us (0.20)
  waiting for transfers between devices: 401 us -> 0 us
  Pallas kernels: 0 us -> 88.3 us
  matrix products: 30.1 us -> 0 us
  between operations: 13.4 us -> 0.01 us
    all_gather x6 -> x0, waiting for transfers between devices: 400 us -> none  [the longest x3 311 us: one_frequency(): lax.all_gather(block, 'rcv', axis=3, tiled=True)]
    pallas_call x0 -> x1, Pallas kernels: none -> 88.3 us  [local(): pl.pallas_call(kernel, out_shape=jax.ShapeDtypeStruct(data.shape, data.dt...]
    dot_general x12 -> x0, matrix products: 30.1 us -> none  [mult(): return jnp.einsum('fsx,fxc->fsc', a, b, preferred_element_type=jnp.float32)]
    dynamic_slice x3 -> x0, local copies, waits for them, and re-layouts: 5.04 us -> none  [local(): return lax.map(one_frequency, data)]
  transfers between devices with their start and end apart: 6 -> 0, of which waited for: 6 -> 0; matrix products, arithmetic and copies ran while one was open for 0% -> 0% of each run, Pallas kernels for 0% -> 0%
where the time goes in v2:
time: 90.4 us; the launch traced here: 90.3 us
  Pallas kernels  88.3 us (98%)
  local copies, waits for them, and re-layouts  2.01 us (2%)
    pallas_call x1, Pallas kernels, local(): pl.pallas_call(kernel, out_shape=jax.ShapeDtypeStruct(data.shape, data.dt...  88.3 us
    unnamed x3, local copies, waits for them, and re-layouts  2.01 us

profile of v2, /device:TPU:1, one launch (start us, length us, event | category | flops | bytes accessed | tf_op | source)
XLA Modules:
  0.0 90.3 jit_solution(17568506217458384808)
XLA Ops:
  0.0 0.0 copy-start
  0.0 1.1 %copy-done = bf16[3,2,512,128]{3,2,1,0:T(8,128)(2,1)S(1)} copy-done((bf16[3,2,512,128]{3,2,1,0:T(8,128)(2,1)S(1)}, bf16[3,2,512,128]{3,2,1,0:T(8,128)(2,1)}, u32[]{:S(2)}) %copy-start) | copy-done | bytes 786456
  1.1 88.3 %shard_map.17 = bf16[3,2,512,128]{3,2,1,0:T(8,128)(2,1)S(1)} custom-call(bf16[3,2,512,128]{3,2,1,0:T(8,128)(2,1)S(1)} %copy-done), custom_call_target="tpu_custom_call" | custom-call | flops 6442450944 | bytes 1572864 | tf_op jit(solution)/shard_map/pallas_call | solution.py:379
  89.4 0.9 copy.3
Async XLA Ops:
  0.0 1.1 %copy-start = (bf16[3,2,512,128]{3,2,1,0:T(8,128)(2,1)S(1)}, bf16[3,2,512,128]{3,2,1,0:T(8,128)(2,1)}, u32[]{:S(2)}) copy-start(bf16[3,2,512,128]{3,2,1,0:T(8,128)(2,1)} %d.1) | copy-start | bytes 2359300

commit v3 on v2

--- a/solution.py
+++ b/solution.py
@@ -13,10 +13,6 @@
 HALF = ROWS // 2
 PARTS = 2
 PIECE = ROWS // PARTS
-
-
-def hops(direction, n):
-    return 4 if direction == n else 3
 
 
 def kernel(d, o, left_a, right_a, left_b, right_b, acc_a, acc_b, part, out_a, out_b,
@@ -33,15 +29,16 @@
     def dev(x, c, z, y):
         return (x * 2 + c, z * NY + y)
 
-    z_next = (dev(x, c, (z + 1) % NZ, y), dev(x, c, (z + NZ - 1) % NZ, y))
-    x_next = (dev((x + 1) % NX, c, z, y), dev((x + NX - 1) % NX, c, z, y))
+    z_next = (dev(x, 0, (z + 1) % NZ, y), dev(x, 0, (z + NZ - 1) % NZ, y))
+    x_next = (dev((x + 1) % NX, 1, z, y), dev((x + NX - 1) % NX, 1, z, y))
     partner = dev(x, 1 - c, z, y)
 
     barrier = pltpu.get_barrier_semaphore()
-    friends = list(z_next) + list(x_next) + [partner]
-    for step in range(1, NY):
-        for core in range(2):
-            friends.append(dev(x, (c + core) % 2, z, (y + step) % NY))
+    friends = [partner]
+    for core in range(2):
+        friends += [dev((x + 1) % NX, (c + core) % 2, z, y), dev((x + NX - 1) % NX, (c + core) % 2, z, y)]
+        friends += [dev(x, (c + core) % 2, (z + 1) % NZ, y), dev(x, (c + core) % 2, (z + NZ - 1) % NZ, y)]
+        friends += [dev(x, (c + core) % 2, z, (y + step) % NY) for step in range(1, NY)]
     for friend in friends:
         pl.semaphore_signal(barrier, inc=1, device_id=friend, device_id_type=MESH)
     acc_a[...] = jnp.zeros_like(acc_a)
@@ -54,14 +51,15 @@
     def got(dst_ref, r_sem):
         pltpu.make_async_copy(dst_ref, dst_ref, r_sem).wait()
 
-    def send(sent, src_ref, dst_ref, s_sem, r_sem, device, here=None):
+    def send(sent, src_ref, dst_ref, s_sem, r_sem, device, here=None, local=True):
         copy = pltpu.make_async_remote_copy(
             src_ref=src_ref, dst_ref=dst_ref, send_sem=s_sem, recv_sem=r_sem, device_id=device, device_id_type=MESH)
         if here is None:
             copy.start()
         else:
             pl.when(jnp.logical_not(here))(copy.start)
-            pl.when(here)(pltpu.make_async_copy(src_ref, dst_ref, r_sem).start)
+            if local:
+                pl.when(here)(pltpu.make_async_copy(src_ref, dst_ref, r_sem).start)
         sent.append((copy, here))
 
     def all_sent(sent):
@@ -73,10 +71,23 @@
 
     first = []
     stays = low == c
+    for direction in range(2):
+        send(first, d.at[1, :, pl.ds(h * HALF, HALF)], right_b.at[x, c, y], xb_s.at[direction, 0, c, 0, 0],
+             xb_r.at[direction, 0, c, 0, 0], x_next[direction])
+    for q in range(PARTS):
+        for direction in range(2):
+            send(first, d.at[1, :, piece(q)], left_b.at[z, y % 2, :, piece(q)], zb_s.at[direction, 0, 0, 0, q],
+                 zb_r.at[direction, 0, 0, 0, q], z_next[direction], low != c, False)
     send(first, d.at[1, :, pl.ds((1 - h) * HALF, HALF)], right_b.at[x, c, y], own_b_s.at[0, 1, 0], own_b_r.at[0, c, 1], dev(x, 1, z, across))
     for q in range(PARTS):
         send(first, d.at[1, :, piece(q)], left_b.at[z, y % 2, :, piece(q)], own_left_s.at[q], own_left_r.at[jnp.where(stays, 0, 1), q],
              dev(x, 0, z, jnp.where(stays, y, pair)), jnp.logical_and(stays, c == 0))
+    for q in range(PARTS):
+        for direction in range(2):
+            send(first, d.at[2 * h, :, piece(q)], left_a.at[z, y, :, piece(q)], za_s.at[direction, 0, 0, 0, q],
+                 za_r.at[direction, 0, 0, 0, q], z_next[direction], low != c, False)
+    for direction in range(2):
+        send(first, d.at[2 * h], right_a.at[x, c, y], xa_s.at[direction, 0, c, 0, 0], xa_r.at[direction, 0, c, 0, 0], x_next[direction])
     send(first, d.at[1, :, pl.ds(h * HALF, HALF)], right_b.at[x, c, y], own_b_s.at[0, 0, 0], own_b_r.at[0, c, 0], dev(x, 1, z, y), c == 1)
     send(first, d.at[2 * (1 - h)], right_a.at[x, c, y], own_a_s.at[0, 1, 0], own_a_r.at[0, c, 1], dev(x, 1, z, across))
     send(first, d.at[2 * h], right_a.at[x, c, y], own_a_s.at[0, 0, 0], own_a_r.at[0, c, 0], dev(x, 1, z, y), c == 1)
@@ -95,8 +106,8 @@
     def block_a(zz, n, m, q):
         return left_a.at[zz, column(n, m), :, piece(q)]
 
-    zb = (block_b, 1, zb_s, zb_r, cb_s, cb_r)
-    za = (block_a, 2, za_s, za_r, ca_s, ca_r)
+    zb = (block_b, zb_s, zb_r, cb_s, cb_r)
+    za = (block_a, za_s, za_r, ca_s, ca_r)
     xb = (right_b, xb_s, xb_r, tb_s, tb_r)
     xa = (right_a, xa_s, xa_r, ta_s, ta_r)
 
@@ -108,41 +119,50 @@
         def at_time(time, action, *args):
             plan.append((time, functools.partial(action, *args)))
 
-        def z_first(block, ms, s_sem, r_sem, c_s, c_r, n, m, q, back):
-            here = block(z, n, m, q)
+        def where(block, direction, t, q):
+            n, other = t // 2, direction if t % 2 == 0 else 1 - direction
+            return (n, 0, other) if block is block_b else (n, other, q)
+
+        def z_first(block, s_sem, r_sem, c_s, c_r, t, q):
             for direction in range(2):
-                give(here, here, s_sem.at[direction, 0, n, m, q], r_sem.at[direction, 0, n, m, q], z_next[direction])
-            if back:
-                give(here, here, c_s.at[0, n, m, q], c_r.at[0, n, m, q], partner)
-
-        def z_arrive(block, ms, s_sem, r_sem, c_s, c_r, step, i, m, q):
+                at = where(block, direction, t, q)
+                here = block(z, *at)
+                if block is block_b and t % 2 == 0:
+                    got(here, own_left_r.at[at[0], at[2]])
+                if at[0] or at[1]:
+                    give(here, here, s_sem.at[direction, 0, *at], r_sem.at[direction, 0, *at], z_next[direction])
+            if block is block_b:
+                give(here, here, c_s.at[0, *at], c_r.at[0, *at], partner)
+
+        def z_arrive(block, s_sem, r_sem, c_s, c_r, step, t, q):
+            came = []
             for direction in range(2):
-                n = direction if i == 0 else 1 - direction
+                at = where(block, direction, t, q)
                 zz = (z + NZ - step) % NZ if direction == 0 else (z + step) % NZ
-                k = NZ - step if direction == 0 else step
-                here = block(zz, n, m, q)
-                got(here, r_sem.at[direction, step - 1, n, m, q])
-                if step < hops(direction, n):
-                    give(here, here, s_sem.at[direction, step, n, m, q], r_sem.at[direction, step, n, m, q], z_next[direction])
-                give(here, here, c_s.at[k, n, m, q], c_r.at[k, n, m, q], partner)
+                here = block(zz, *at)
+                got(here, r_sem.at[direction, step - 1, *at])
+                if step < 4 - t % 2:
+                    give(here, here, s_sem.at[direction, step, *at], r_sem.at[direction, step, *at], z_next[direction])
+                came.append((here, NZ - step if direction == 0 else step, at))
+            for here, k, at in came:
+                give(here, here, c_s.at[k, *at], c_r.at[k, *at], partner)
 
         def start_b(n):
-            for q in range(PARTS):
-                got(block_b(z, n, 0, q), own_left_r.at[n, q])
-                z_first(*zb, n, 0, q, True)
+            for t in (2 * n, 2 * n + 1):
+                z_first(*zb, t, 0)
 
         def take_a(n, m):
             got(left_a.at[z, column(n, m)], give_r.at[n, m])
 
         def start_a(n, q):
-            for m in range(2):
-                z_first(*za, n, m, q, False)
+            for t in (2 * n, 2 * n + 1):
+                z_first(*za, t, q)
 
         def left_ready(z_of, k, q):
-            block, ms, _, _, _, c_r = z_of
-            if core == 1 and (k or ms == 1):
+            block, _, _, _, c_r = z_of
+            if core == 1 and (k or block is block_b):
                 for n in range(2):
-                    for m in range(ms):
+                    for m in range(1 if block is block_b else 2):
                         got(block((z + k) % NZ, n, m, q), c_r.at[k, n, m, q])
 
         def own_second(right, s_sem, r_sem, k, m):
@@ -160,7 +180,7 @@
         def x_first(right, s_sem, r_sem, t_s, t_r, n, m):
             for k in range(2):
                 here = right.at[x, k, column(n, m)]
-                for direction in range(2):
+                for direction in range(2 if n or m else 0):
                     give(here, here, s_sem.at[direction, 0, k, n, m], r_sem.at[direction, 0, k, n, m], x_next[direction])
                 if m == 1:
                     pass_on(right, t_s, t_r, 0, x, k, n)
@@ -268,25 +288,28 @@
 
         hop = 1.9
         sub = 39.4 / PARTS
-        begin_b = 1.7
-        begin_a = begin_b + 19.7
-
-        def z_time_b(step, i, q):
-            return begin_b + 5.6 * (step - 1) + 2.8 * (i + (q + 1) / PARTS) + hop
-
-        def z_time_a(step, i, m, q):
-            if q < PARTS - 2:
-                return begin_a + sub * (q + (step - 1 + (2 * i + m + 1) / 4) / 3.5) + hop
-            ahead = sub / 3.5
-            if q == PARTS - 2:
-                return begin_a + sub * (q + (step - 1 + (2 * i + m + 1) / 4) / 3.5) + hop + (ahead if step > 1 else 0)
+        begin_b = 3.1
+        begin_a = 21.4
+
+        ahead = sub / 3.5
+
+        def done_of(step, t):
+            return (t + 1 if step < 4 else t // 2 + 1) / 4
+
+        def z_time_b(step, t):
+            return (begin_b if step > 1 or t > 1 else 0.3) + 5.6 * (step - 1 + done_of(step, t)) + hop
+
+        def z_time_a(step, t, q):
+            if q < PARTS - 1:
+                late_by = ahead if q == PARTS - 2 and step > 1 else 0
+                return begin_a + sub * q + ahead * (step - 1 + done_of(step, t)) + hop + late_by
             if step == 1:
-                return begin_a + sub * q + ahead * (1 + (2 * i + m) / 4) - 2.5
-            return begin_a + sub * q + ahead * (step - 1 + (2 * i + m + 1) / 4) + hop
+                return begin_a + sub * q + ahead * (1 + t / 4) - 2.5
+            return begin_a + sub * q + ahead * (step - 1 + done_of(step, t)) + hop
 
         if core == 0:
-            at_time(1, start_b, 0)
-            at_time(4.5, start_b, 1)
+            at_time(3, start_b, 0)
+            at_time(5, start_b, 1)
             for m in range(2):
                 at_time(17.4 + m / 100, take_a, 0, m)
                 at_time(21.5 + m / 100, take_a, 1, m)
@@ -295,11 +318,10 @@
                 at_time(max(17.5, first_time), start_a, 0, q)
                 at_time(max(21.6, first_time + 0.01), start_a, 1, q)
             for step in range(1, 5):
-                for i in range(2 if step < 4 else 1):
+                for t in range(4) if step < 4 else (0, 2):
+                    at_time(z_time_b(step, t), z_arrive, *zb, step, t, 0)
                     for q in range(PARTS):
-                        at_time(z_time_b(step, i, q), z_arrive, *zb, step, i, 0, q)
-                        for m in range(2):
-                            at_time(z_time_a(step, i, m, q), z_arrive, *za, step, i, m, q)
+                        at_time(z_time_a(step, t, q), z_arrive, *za, step, t, q)
         else:
             for k in range(2):
                 at_time(1.5, own_second, right_b, own_b_s, own_b_r, k, 0)
@@ -321,37 +343,39 @@
             at_time(4.7, x_first, *xb, 0, 1)
             at_time(7.7, x_first, *xb, 1, 0)
             at_time(11.1, x_first, *xb, 1, 1)
-            at_time(15.8, x_first, *xa, 0, 0)
-            at_time(15.9, x_first, *xa, 0, 1)
+            at_time(17.3, x_first, *xa, 0, 0)
+            at_time(17.31, x_first, *xa, 0, 1)
             at_time(23.6, x_first, *xa, 1, 0)
             at_time(23.7, x_first, *xa, 1, 1)
             for k in range(2):
+                at_time(5.2, x_arrive, *xb, k, 0, 0)
+                at_time(8.7 + 1.4 * (k + 1) + hop, x_arrive, *xb, k, 0, 1)
+                at_time(27, x_arrive, *xa, k, 0, 0)
+                at_time(22.7 + 2.8 * (k + 1) + hop, x_arrive, *xa, k, 0, 1)
                 for m in range(2):
                     nth = 2 * m + k + 1
-                    at_time(2 + 1.4 * nth + hop, x_arrive, *xb, k, 0, m)
-                    at_time(8 + 1.4 * nth + hop, x_arrive, *xb, k, 1, m)
-                    at_time(14 + 1.4 * nth + hop, x_last, *xb, k, m)
-                    at_time(19.5 + 2.8 * nth + hop, x_arrive, *xa, k, 0, m)
-                    at_time(31 + 2.8 * nth + hop, x_arrive, *xa, k, 1, m)
-                    at_time(42.5 + 2.8 * nth + hop, x_last, *xa, k, m)
+                    at_time(11.5 + 1.4 * nth + hop, x_arrive, *xb, k, 1, m)
+                    at_time(17.1 + 1.4 * nth + hop, x_last, *xb, k, m)
+                    at_time(28.3 + 2.8 * nth + hop, x_arrive, *xa, k, 1, m)
+                    at_time(39.6 + 2.8 * nth + hop, x_last, *xa, k, m)
             at_time(46.8, keep_left)
-        at_time(25.2, whole_b)
-        at_time(43, finish_b)
-        at_time(47, right_ready, xa, range(3))
-        late = 56.5
+        at_time(29, whole_b)
+        at_time(50, finish_b)
+        at_time(53, right_ready, xa, range(3))
+        late = 60
         at_time(late, right_ready, xa, (3,))
         for q in range(PARTS):
-            done = z_time_a(4, 0, 1, q) + 0.2
+            done = z_time_a(4, 2, q) + 0.2
             if done < 49:
-                at_time(max(done, 47.1), chunks_a, -3, 4, q, False)
+                at_time(max(done, 53.1), chunks_a, -3, 4, q, False)
                 at_time(late, far_a, q)
                 at_time(late + 0.01, finish_a, q)
             elif done < late + 1:
                 at_time(late + 0.02, chunks_a, -3, 4, q)
                 at_time(late + 0.03, finish_a, q)
             else:
-                at_time(max(late + 0.04, z_time_a(2, 1, 1, q) + 0.2), chunks_a, -2, 2, q)
-                third = z_time_a(3, 1, 1, q) + 0.2
+                at_time(max(late + 0.04, z_time_a(2, 3, q) + 0.2), chunks_a, -2, 2, q)
+                third = z_time_a(3, 3, q) + 0.2
                 at_time(third, chunks_a, -3, -3, q)
                 at_time(third, chunks_a, 3, 3, q)
                 at_time(done, chunks_a, 4, 4, q)

time: 90.4 us -> 86.4 us (0.956)
  Pallas kernels: 88.3 us -> 84.3 us
    pallas_call x1, Pallas kernels: 88.3 us -> 84.3 us  [local(): pl.pallas_call(kernel, out_shape=jax.ShapeDtypeStruct(data.shape, data.dt...]
where the time goes in v3:
time: 86.4 us; the launch traced here: 86.3 us
  Pallas kernels  84.3 us (98%)
  local copies, waits for them, and re-layouts  2.01 us (2%)
    pallas_call x1, Pallas kernels, local(): pl.pallas_call(kernel, out_shape=jax.ShapeDtypeStruct(data.shape, data.dt...  84.3 us
    unnamed x3, local copies, waits for them, and re-layouts  2.01 us

profile of v3, /device:TPU:1, one launch (start us, length us, event | category | flops | bytes accessed | tf_op | source)
XLA Modules:
  0.0 86.3 jit_solution(2738339925326815388)
XLA Ops:
  0.0 0.0 copy-start
  0.0 1.1 %copy-done = bf16[3,2,512,128]{3,2,1,0:T(8,128)(2,1)S(1)} copy-done((bf16[3,2,512,128]{3,2,1,0:T(8,128)(2,1)S(1)}, bf16[3,2,512,128]{3,2,1,0:T(8,128)(2,1)}, u32[]{:S(2)}) %copy-start) | copy-done | bytes 786456
  1.1 84.3 %shard_map.17 = bf16[3,2,512,128]{3,2,1,0:T(8,128)(2,1)S(1)} custom-call(bf16[3,2,512,128]{3,2,1,0:T(8,128)(2,1)S(1)} %copy-done), custom_call_target="tpu_custom_call" | custom-call | flops 6442450944 | bytes 1572864 | tf_op jit(solution)/shard_map/pallas_call | solution.py:403
  85.4 0.9 %copy.3 = bf16[3,2,512,128]{3,2,1,0:T(8,128)(2,1)} copy(bf16[3,2,512,128]{3,2,1,0:T(8,128)(2,1)S(1)} %shard_map.17) | data formatting | bytes 1572864
Async XLA Ops:
  0.0 1.1 %copy-start = (bf16[3,2,512,128]{3,2,1,0:T(8,128)(2,1)S(1)}, bf16[3,2,512,128]{3,2,1,0:T(8,128)(2,1)}, u32[]{:S(2)}) copy-start(bf16[3,2,512,128]{3,2,1,0:T(8,128)(2,1)} %d.1) | copy-start | bytes 2359300

commit v4 on v3

--- a/solution.py
+++ b/solution.py
@@ -403,7 +403,7 @@
     return pl.pallas_call(
         kernel,
         out_shape=jax.ShapeDtypeStruct(data.shape, data.dtype),
-        in_specs=[pl.BlockSpec(memory_space=pltpu.VMEM)],
+        in_specs=[pl.BlockSpec(memory_space=pltpu.HBM)],
         out_specs=pl.BlockSpec(memory_space=pltpu.VMEM),
         scratch_shapes=[
             pltpu.VMEM((NZ, 4, 2, ROWS, COLS), bf16),

time: 86.4 us -> 86.4 us (level)
  no operation moved by 1% of the time
where the time goes in v4:
time: 86.4 us; the launch traced here: 86.3 us
  Pallas kernels  84.3 us (98%)
  local copies, waits for them, and re-layouts  2.01 us (2%)
    pallas_call x1, Pallas kernels, local(): pl.pallas_call(kernel, out_shape=jax.ShapeDtypeStruct(data.shape, data.dt...  84.3 us
    unnamed x3, local copies, waits for them, and re-layouts  2.01 us

profile of v4, /device:TPU:1, one launch (start us, length us, event | category | flops | bytes accessed | tf_op | source)
XLA Modules:
  0.0 86.3 jit_solution(2738339925326815388)
XLA Ops:
  0.0 0.0 copy-start
  0.0 1.1 %copy-done = bf16[3,2,512,128]{3,2,1,0:T(8,128)(2,1)S(1)} copy-done((bf16[3,2,512,128]{3,2,1,0:T(8,128)(2,1)S(1)}, bf16[3,2,512,128]{3,2,1,0:T(8,128)(2,1)}, u32[]{:S(2)}) %copy-start) | copy-done | bytes 786456
  1.1 84.3 %shard_map.17 = bf16[3,2,512,128]{3,2,1,0:T(8,128)(2,1)S(1)} custom-call(bf16[3,2,512,128]{3,2,1,0:T(8,128)(2,1)S(1)} %copy-done), custom_call_target="tpu_custom_call" | custom-call | flops 6442450944 | bytes 1572864 | tf_op jit(solution)/shard_map/pallas_call | solution.py:403
  85.4 0.9 %copy.3 = bf16[3,2,512,128]{3,2,1,0:T(8,128)(2,1)} copy(bf16[3,2,512,128]{3,2,1,0:T(8,128)(2,1)S(1)} %shard_map.17) | data formatting | bytes 1572864
Async XLA Ops:
  0.0 1.1 %copy-start = (bf16[3,2,512,128]{3,2,1,0:T(8,128)(2,1)S(1)}, bf16[3,2,512,128]{3,2,1,0:T(8,128)(2,1)}, u32[]{:S(2)}) copy-start(bf16[3,2,512,128]{3,2,1,0:T(8,128)(2,1)} %d.1) | copy-start | bytes 2359300
